TPU v7x, 256 devices: a whole 4x4x8 slice. The times are simulated.
256 devices in a mesh: pipe: 8 (over y_lo, x), fsdp: 32 (over z, y_hi, core).
Axes of the slice: x: 4, y: 4 (y_hi: 2, y_lo: 2; y = y_hi * 2 + y_lo), z: 8, core: 2. Of those that a mesh axis runs over, the one named last changes fastest.
Arguments:
- tokens: bfloat16 [512, 12288], P(None, 'pipe'), may hold values from -6 to 6
- cotangent: bfloat16 [512, 12288], P(None, 'pipe'), may hold values from -6 to 6
- gate_weight: bfloat16 [12288, 28672], P('pipe', 'fsdp'), may hold values from -0.0546875 to 0.0546875
- up_weight: bfloat16 [12288, 28672], P('pipe', 'fsdp'), may hold values from -0.0546875 to 0.0546875
- down_weight: bfloat16 [28672, 12288], P('fsdp', 'pipe'), may hold values from -0.0546875 to 0.0546875
- adapter_down_first: bfloat16 [28672, 64], P('fsdp'), may hold values from -0.03125 to 0.03125
- adapter_down_second: bfloat16 [64, 12288], P(None, 'pipe'), may hold values from -0.29882812 to 0.29882812
Outputs:
- grad_input: bfloat16 [512, 12288], P('fsdp', 'pipe')
- grad_lora_a: float32 [28672, 64], P('fsdp')
- grad_lora_b: float32 [64, 12288], P(None, 'pipe')
All inputs are finite; a program needn't handle non-finite values.
Results may differ from a plain program's by a relative error of at most 0.005.
Values may be sent and summed in bfloat16 or wider, within the bound.
A program may use at most 64 MiB of HBM per device.

v0:
```python
import jax
import jax.numpy as jnp
from jax import lax
from jax.sharding import PartitionSpec as P

adapter_scale = 0.5


def contract_trailing(left, right):
    return lax.dot_general(
        left, right, (((1,), (1,)), ((), ())), preferred_element_type=jnp.float32
    )


def contract_leading(left, right):
    return lax.dot_general(
        left, right, (((0,), (0,)), ((), ())), preferred_element_type=jnp.float32
    )


def activate(gate, up_values):
    sigmoid_gate = jax.nn.sigmoid(gate)
    silu_gate = gate * sigmoid_gate
    return (sigmoid_gate, silu_gate, (silu_gate * up_values).astype(jnp.bfloat16))


def pre_grads(hidden_gradient, gate, up_values, sigmoid_gate, silu_gate):
    grad_gate = (
        hidden_gradient * up_values * sigmoid_gate * (1.0 + gate * (1.0 - sigmoid_gate))
    ).astype(jnp.bfloat16)
    grad_up = (hidden_gradient * silu_gate).astype(jnp.bfloat16)
    return (grad_gate, grad_up)


def shards(
    tokens, cotangent, gate_weight, up_weight, down_weight, adapter_down_first, adapter_down_second
):
    gate_part = jnp.dot(tokens, gate_weight, preferred_element_type=jnp.float32)
    up_part = jnp.dot(tokens, up_weight, preferred_element_type=jnp.float32)
    hgrad_part = contract_trailing(cotangent, down_weight)
    backward_piece = contract_trailing(cotangent, adapter_down_second)
    gate, up_values = lax.psum((gate_part, up_part), "pipe")
    sigmoid_gate, silu_gate, hidden_activation = activate(gate, up_values)
    hidden_gradient_sum, back_sum = lax.psum((hgrad_part, backward_piece), "pipe")
    backward_lowrank = back_sum.astype(jnp.bfloat16)
    hidden_gradient = hidden_gradient_sum + adapter_scale * contract_trailing(
        backward_lowrank, adapter_down_first
    )
    grad_gate, grad_up = pre_grads(hidden_gradient, gate, up_values, sigmoid_gate, silu_gate)
    lowrank_piece = jnp.dot(
        hidden_activation, adapter_down_first, preferred_element_type=jnp.float32
    )
    lowrank_product = lax.psum(lowrank_piece, "fsdp").astype(jnp.bfloat16)
    grad_input = lax.psum_scatter(
        contract_trailing(grad_gate, gate_weight) + contract_trailing(grad_up, up_weight),
        "fsdp",
        scatter_dimension=0,
        tiled=True,
    ).astype(jnp.bfloat16)
    gradient_factor_first = adapter_scale * contract_leading(hidden_activation, backward_lowrank)
    gradient_factor_second = adapter_scale * contract_leading(lowrank_product, cotangent)
    return (grad_input, gradient_factor_first, gradient_factor_second)


def solution(mesh):
    return jax.shard_map(
        shards,
        mesh=mesh,
        in_specs=(
            P(None, "pipe"),
            P(None, "pipe"),
            P("pipe", "fsdp"),
            P("pipe", "fsdp"),
            P("fsdp", "pipe"),
            P("fsdp", None),
            P(None, "pipe"),
        ),
        out_specs=(P("fsdp", "pipe"), P("fsdp", None), P(None, "pipe")),
        check_vma=False,
    )
```

profile of v0, /device:TPU:24, one launch (start us, length us, event | category | flops | bytes accessed | tf_op | source)
XLA Modules:
  0.0 314.1 jit_solution(15638665704601529106)
XLA Ops:
  7.2 0.0 copy-start
  7.2 0.0 all-reduce.5.cloned.1.call-start
  7.2 5.4 %fusion.11 = f32[512,896]{1,0:T(8,128)} fusion(bf16[512,1536]{1,0:T(8,128)(2,1)} %param.7, bf16[1536,896]{1,0:T(8,128)(2,1)} %param.10), kind=kOutput, calls=%fused_computation.18 | convolution fusion | flops 1409286144 | bytes 6160384 | tf_op jit(solution)/shard_map/dot_general | solution.py:39
  12.7 3.1 fusion.12
  15.8 3.1 fusion.9
  18.9 0.0 all-reduce.5.cloned.1.call-update
  18.9 0.0 copy-start.5
  18.9 0.0 reduce-scatter.2.cloned.1.call-start
  19.0 0.8 copy-done.6
  19.8 2.0 fusion.10
  21.8 37.4 %all-reduce.6 = bf16[512,64]{0,1:T(8,128)(2,1)S(1)} all-reduce(f32[512,64]{0,1:T(8,128)S(1)} %fusion.10), channel_id=1, replica_groups=mesh['pipe'=8,'fsdp'=32] {'pipe'}, use_global_device_ids=true, to_apply=%region_1.0 | all-reduce | flops 32768 | bytes 196608 | tf_op jit(solution)/shard_map/psum | solution.py:44
  59.2 99.2 %all-reduce.5.cloned.1.call-done = (f32[512,896]{1,0:T(8,128)}, f32[512,896]{1,0:T(8,128)}, f32[512,896]{1,0:T(8,128)}) async-done(((f32[512,896]{1,0:T(8,128)}, f32[512,896]{1,0:T(8,128)}, f32[512,896]{1,0:T(8,128)}), (f32[512,896]{1,0:T(8,128)}, f32[512,896]{1,0:T(8,128)}, f32[512,896]{1,0:T(8,128)})) %all-reduce.5.cloned.1.call-update) | async-done | bytes 5505040 | tf_op jit(solution)/shard_map/psum | solution.py:42
  158.4 2.1 multiply_add_fusion
  160.5 0.5 copy-done.4
  161.0 2.3 fusion.1
  163.3 3.5 %convolution_add_fusion = f32[512,1536]{1,0:T(8,128)} fusion(f32[512,1536]{1,0:T(8,128)S(1)} %fusion.1, bf16[1536,896]{1,0:T(8,128)(2,1)S(1)} %copy-done.8, f32[512,896]{1,0:T(8,128)S(1)} %multiply_add_fusion, f32[512,896]{1,0:T(8,128)S(1)} %copy-done.3), kind=kOutput, calls=%fused_computation | convolution fusion | flops 1412825088 | bytes 12713984 | tf_op jit(solution)/shard_map/dot_general | solution.py:10
  166.8 0.0 reduce-scatter.2.cloned.1.call-update
  166.9 2.6 multiply_convert_fusion
  169.4 0.9 copy-done.1
  170.4 0.4 fusion.13
  170.8 130.2 %all-reduce.7 = bf16[512,64]{1,0:T(8,128)(2,1)S(1)} all-reduce(f32[512,64]{1,0:T(8,128)S(1)} %fusion.13), channel_id=1, replica_groups=mesh['pipe'=8,'fsdp'=32] {'fsdp'}, use_global_device_ids=true, to_apply=%region_5.0 | all-reduce | flops 32768 | bytes 196608 | tf_op jit(solution)/shard_map/psum | solution.py:53
  301.0 2.2 convolution_multiply_fusion.1
  303.1 2.6 convolution_multiply_fusion
  305.7 1.5 convert_element_type.21
  (16 shorter events, 0.0 us)
Async XLA Ops:
  7.2 5.5 %copy-start = (bf16[1536,896]{1,0:T(8,128)(2,1)S(1)}, bf16[1536,896]{1,0:T(8,128)(2,1)}, u32[]{:S(2)}) copy-start(bf16[1536,896]{1,0:T(8,128)(2,1)} %param.9) | copy-start | bytes 8257540
  7.2 151.2 %all-reduce.5.cloned.1.call-start = ((), (), s32[]{:S(2)}) async-start(), calls=%async_computation.2 | async-start | bytes 11010048 | tf_op jit(solution)/shard_map/psum | solution.py:42
  7.2 5.5 %copy-start.9 = (bf16[512,1536]{1,0:T(8,128)(2,1)S(1)}, bf16[512,1536]{1,0:T(8,128)(2,1)}, u32[]{:S(2)}) copy-start(bf16[512,1536]{1,0:T(8,128)(2,1)} %param.7) | copy-start | bytes 4718596
  12.7 3.1 copy-start.2
  12.7 3.1 copy-start.7
  18.9 0.9 copy-start.6
  18.9 139.5 %copy-start.5 = (bf16[896,64]{0,1:T(8,128)(2,1)S(1)}, bf16[896,64]{0,1:T(8,128)(2,1)}, u32[]{:S(2)}) copy-start(bf16[896,64]{0,1:T(8,128)(2,1)} %param.12) | copy-start | bytes 344068
  18.9 286.8 %reduce-scatter.2.cloned.1.call-start = ((), (), s32[]{:S(2)}) async-start(), calls=%async_computation.1 | async-start | bytes 3244032 | tf_op jit(solution)/shard_map/reduce_scatter | solution.py:54
  158.4 2.1 copy-start.3
  158.4 2.6 copy-start.4
  161.0 2.3 copy-start.8
  169.4 1.0 copy-start.1
Sparse Core Ops, SparseCore 0:
  19.0 139.3 all-reduce.4
  167.0 122.1 reduce-scatter.1
where the time goes:
time: 319 us; the launch traced here: 314 us
  blocking collectives  168 us (53%)
  waiting for transfers between devices  99.3 us (31%)
  matrix products  26.6 us (8%)
  between operations  14.1 us (4%)
  other arithmetic  4.09 us (1%)
    psum x1, blocking collectives, shards(): lowrank_product = lax.psum(lowrank_piece, 'fsdp').astype(jnp.bfloat16)  130 us
    psum x1, waiting for transfers between devices, shards(): gate, up_values = lax.psum((gate_part, up_part), 'pipe')  99.2 us
    psum x1, blocking collectives, shards(): lax.psum((hgrad_part, backward_piece), 'pipe')  37.4 us
    dot_general x5, matrix products, contract_trailing(): lax.dot_general(left, right, (((1,), (1,)), ((), ())), preferred_element_...  13 us
  transfers between devices with their start and end apart: 2, of which 1 were waited for; matrix products, arithmetic and copies ran while one was open for 3% of the time, Pallas kernels for 0%

commit v1 on v0

v1 whole, which is shorter than its diff:
```python
import jax
import jax.numpy as jnp
from jax import lax
from jax.experimental import pallas as pl
from jax.experimental.pallas import tpu as pltpu
from jax.sharding import PartitionSpec as P

F32 = jnp.float32
BF16 = jnp.bfloat16
MESH = pl.DeviceIdType.MESH

TOK = 512
FEAT = 1536
HID = 896
RANK = 64
BATCHES = 4
ROWS = 128
BLK = 16
XW = 512
YW = 384
SPLIT = (0, 640, 1152)
N_COPIES = 200
N_LOADS = 20


def dot(a, b):
    return jnp.dot(a, b, preferred_element_type=F32)


def dot_t(a, b):
    return lax.dot_general(a, b, (((1,), (1,)), ((), ())), preferred_element_type=F32)


def dot_lead(a, b):
    return lax.dot_general(a, b, (((0,), (0,)), ((), ())), preferred_element_type=F32)


def pack(v):
    return jnp.concatenate([v[:32], v[32:]], axis=1)


def unpack(v):
    return jnp.concatenate([v[:, :64], v[:, 64:]], axis=0)


class Bag:
    pass


class Copies:
    def __getattr__(self, name):
        made = {}
        setattr(self, name, made)
        return made


def scratch_spec():
    specs = []
    v = Bag()

    def new(shape, dtype):
        specs.append(pltpu.VMEM(shape, dtype))
        return len(specs) - 1

    n = BATCHES
    v.tok = new((n, 8, BLK, FEAT), BF16)
    v.cot = new((n, 8, BLK, FEAT), BF16)
    v.gw = new((FEAT, HID), BF16)
    v.uw = new((FEAT, HID), BF16)
    v.dw = new((HID, FEAT), BF16)
    v.down_a = new((RANK, HID), BF16)
    v.down_b = new((RANK, FEAT), BF16)
    wide = 3 * XW
    v.xpart = new((n, ROWS, wide), F32)
    v.xfd_s = new((n, 4, BLK, wide), BF16)
    v.xfd_r = new((n, 4, BLK, wide), BF16)
    v.xc_s = new((n, 2, BLK, wide), BF16)
    v.xc_r = new((n, 2, BLK, wide), BF16)
    v.xsum = new((n, 2, BLK, wide), F32)
    v.xy_s = new((n, BLK, wide), BF16)
    v.xy_r = new((n, BLK, wide), BF16)
    v.xgrad = new((n, ROWS, 2 * XW), BF16)
    wide = 3 * YW
    v.ypart = new((n, ROWS, wide), F32)
    v.yy_s = new((n, 64, wide), BF16)
    v.yy_r = new((n, 64, wide), BF16)
    v.ysum = new((n, 64, wide), F32)
    v.yfd_s = new((n, 2, BLK, wide), BF16)
    v.yfd_r = new((n, 2, BLK, wide), BF16)
    v.yc_s = new((n, BLK, wide), BF16)
    v.yc_r = new((n, BLK, wide), BF16)
    v.ygrad = new((n, ROWS, 2 * YW), BF16)
    v.hidden = new((TOK // 8, HID), BF16)
    v.acc = new((n, ROWS, FEAT), F32)
    v.back = new((n, 8, BLK, RANK), F32)
    v.back_s = new((8, 32, 128), BF16)
    v.back_r = new((8, 32, 128), BF16)
    v.la_s = new((RANK, HID), F32)
    v.la_r = new((8, 8, HID), F32)
    v.la = new((RANK, HID), F32)
    v.low_s = new((32, 128), F32)
    v.low_cr = new((32, 128), F32)
    v.low_h = new((16, 128), F32)
    v.low_zr = new((16, 16, 128), F32)
    v.low_p = new((2, 8, 16, 128), BF16)
    v.core_r = new((n, ROWS, FEAT), F32)
    v.z_s = new((n, 8, BLK, FEAT), BF16)
    v.z_r = new((n, 8, BLK, FEAT), BF16)
    v.yh_s = new((n, BLK, FEAT), F32)
    v.yh_r = new((n, BLK, FEAT), F32)
    return specs, v


def kernel(*refs):
    specs, places = scratch_spec()
    tok_h, cot_h, gw_h, uw_h, dw_h, a_h, b_h, gi_o, la_o, lb_o = refs[:10]
    held = refs[10 : 10 + len(specs)]
    send_sems, recv_sems, load_sems = refs[10 + len(specs) :]
    S = Bag()
    for name, place in vars(places).items():
        setattr(S, name, held[place])

    p = lax.axis_index("pipe")
    f = lax.axis_index("fsdp")
    x = lax.rem(p, 4)
    y = lax.div(p, 4)
    z = lax.div(f, 4)
    yh = lax.rem(lax.div(f, 2), 2)
    core = lax.rem(f, 2)
    chip = lax.div(f, 2)
    x_p, x_m, x_f = lax.rem(x + 1, 4), lax.rem(x + 3, 4), lax.rem(x + 2, 4)

    def pipe(i):
        return {"pipe": i}

    def fsdp(i):
        return {"fsdp": i}

    to_xp = pipe(y * 4 + x_p)
    to_xm = pipe(y * 4 + x_m)
    to_y = pipe((1 - y) * 4 + x)
    to_core = fsdp(f + 1 - 2 * core)
    to_yh = fsdp(f + 2 - 4 * yh)

    count = [0]
    sent = []

    def remote(src, dst, dev):
        i = count[0]
        count[0] += 1
        return pltpu.make_async_remote_copy(
            src_ref=src,
            dst_ref=dst,
            send_sem=send_sems.at[i],
            recv_sem=recv_sems.at[i],
            device_id=dev,
            device_id_type=MESH,
        )

    def go(cp, cond=None):
        cp.start()
        sent.append((cp, cond))
        return cp

    loads = {}

    def load(key, dst, src):
        cp = pltpu.make_async_copy(src, dst, load_sems.at[len(loads)])
        cp.start()
        loads[key] = cp

    XC, YC = slice(0, XW), slice(XW, HID)
    xcols, ycols = pl.ds(0, XW), pl.ds(XW, YW)
    TOKENS, COT, GATE_W, UP_W, DOWN_W, DOWN_A, DOWN_B = range(7)
    load((TOKENS, 0), S.tok.at[0], tok_h.at[:, 0])
    load((GATE_W, 0), S.gw.at[:, xcols], gw_h.at[:, xcols])
    load((UP_W, 0), S.uw.at[:, xcols], uw_h.at[:, xcols])
    load((COT, 0), S.cot.at[0], cot_h.at[:, 0])
    load(DOWN_B, S.down_b, b_h)
    load(DOWN_A, S.down_a, a_h)
    load((DOWN_W, 0), S.dw.at[xcols], dw_h.at[xcols])
    load((GATE_W, 1), S.gw.at[:, ycols], gw_h.at[:, ycols])
    load((UP_W, 1), S.uw.at[:, ycols], uw_h.at[:, ycols])
    load((DOWN_W, 1), S.dw.at[ycols], dw_h.at[ycols])
    for i in range(1, BATCHES):
        load((TOKENS, i), S.tok.at[i], tok_h.at[:, i])
        load((COT, i), S.cot.at[i], cot_h.at[:, i])

    barrier = pltpu.get_barrier_semaphore()
    peers = [pipe(lax.rem(p + j, 8)) for j in range(1, 8)]
    peers += [to_core]
    peers += [fsdp(lax.rem(chip + j, 16) * 2 + core) for j in range(1, 16)]
    for dev in peers:
        pl.semaphore_signal(barrier, inc=1, device_id=dev, device_id_type=MESH)

    def block(x_, y_):
        return pl.ds(pl.multiple_of((y_ * 4 + x_) * BLK, BLK), BLK)

    def quarter(x_):
        return pl.ds(pl.multiple_of(x_ * BLK, BLK), BLK)

    def half(y_):
        return pl.ds(pl.multiple_of(y_ * 64, 64), 64)

    def side(k):
        return slice(SPLIT[k], SPLIT[k + 1])

    def side_d(k):
        return pl.ds(SPLIT[k], SPLIT[k + 1] - SPLIT[k])

    st = Copies()

    def whole(ref, i):
        return ref[i].reshape(ROWS, FEAT)

    def products(i, part, cols, w):
        tok, cot = whole(S.tok, i), whole(S.cot, i)
        part[i, :, 0:w] = dot(tok, S.gw[:, cols])
        part[i, :, w : 2 * w] = dot(tok, S.uw[:, cols])
        back = (0.5 * S.back[i].reshape(ROWS, RANK)).astype(BF16)
        part[i, :, 2 * w :] = dot_t(cot, S.dw[cols, :]) + dot(back, S.down_a[:, cols])

    def a1(i):
        if i == 0:
            for key in ((TOKENS, 0), (COT, 0), DOWN_A, DOWN_B):
                loads[key].wait()
            for kind in (GATE_W, UP_W, DOWN_W):
                loads[kind, 0].wait()
        else:
            loads[TOKENS, i].wait()
            loads[COT, i].wait()
        S.back[i] = dot_t(whole(S.cot, i), S.down_b[...]).reshape(8, BLK, RANK)
        products(i, S.xpart, XC, XW)
        if i == 0:
            pl.semaphore_wait(barrier, len(peers))
        plan = ((x_f, 0, to_xp), (x_f, 1, to_xm), (x_p, 1, to_xp), (x_m, 0, to_xm))
        for k, (bx, by, dev) in enumerate(plan):
            S.xfd_s[i, k] = S.xpart[i, block(bx, by), :].astype(BF16)
            st.xfd[i, k] = go(remote(S.xfd_s.at[i, k], S.xfd_r.at[i, k], dev))
        if i == 0:
            for kind in (GATE_W, UP_W, DOWN_W):
                loads[kind, 1].wait()
        products(i, S.ypart, YC, YW)
        S.yy_s[i] = S.ypart[i, half(1 - y), :].astype(BF16)
        st.yy[i] = go(remote(S.yy_s.at[i], S.yy_r.at[i], to_y))

    def a2(i):
        for k, rows, dev in ((0, block(x_p, 0), to_xp), (1, block(x_m, 1), to_xm)):
            st.xfd[i, k].wait_recv()
            S.xc_s[i, k] = (S.xpart[i, rows, :] + S.xfd_r[i, k].astype(F32)).astype(BF16)
            st.xc[i, k] = go(remote(S.xc_s.at[i, k], S.xc_r.at[i, k], dev))
        st.yy[i].wait_recv()
        S.ysum[i] = S.ypart[i, half(y), :] + S.yy_r[i].astype(F32)
        plan = ((0, 0, x_f, to_xp), (0, 1, x_f, to_xm), (1, 1, x_p, to_xp), (1, 0, x_m, to_xm))
        for k, s, bx, dev in plan:
            S.yfd_s[i, k, :, side(s)] = S.ysum[i, quarter(bx), side(s)].astype(BF16)
            st.yfd[i, k, s] = go(
                remote(
                    S.yfd_s.at[i, k, :, side_d(s)], S.yfd_r.at[i, k, :, side_d(s)], dev
                )
            )

    def a3(i):
        for k in (2, 3):
            st.xfd[i, k].wait_recv()
        for k in (0, 1):
            st.xc[i, k].wait_recv()
        for k in (0, 1):
            S.xsum[i, k] = (
                S.xpart[i, block(x, k), :]
                + S.xfd_r[i, 3 - k].astype(F32)
                + S.xc_r[i, k].astype(F32)
            )
        S.xy_s[i] = S.xsum[i, 1 - y].astype(BF16)
        st.xy[i] = go(remote(S.xy_s.at[i], S.xy_r.at[i], to_y))
        for s, bx, dev in ((0, x_p, to_xp), (1, x_m, to_xm)):
            st.yfd[i, 0, s].wait_recv()
            S.yc_s[i, :, side(s)] = (
                S.ysum[i, quarter(bx), side(s)] + S.yfd_r[i, 0, :, side(s)].astype(F32)
            ).astype(BF16)
            st.yc[i, s] = go(
                remote(S.yc_s.at[i, :, side_d(s)], S.yc_r.at[i, :, side_d(s)], dev)
            )

    def activate(i, total, w, grad, cols):
        gate, up, hg = total[:, :w], total[:, w : 2 * w], total[:, 2 * w :]
        sig = jax.nn.sigmoid(gate)
        silu = gate * sig
        mine = block(x, y)
        grad[i, mine, 0:w] = (hg * up * sig * (1.0 + gate * (1.0 - sig))).astype(BF16)
        grad[i, mine, w : 2 * w] = (hg * silu).astype(BF16)
        S.hidden[i * BLK : (i + 1) * BLK, cols] = (silu * up).astype(BF16)

    def a4(i):
        st.xy[i].wait_recv()
        activate(i, S.xsum[i, y] + S.xy_r[i].astype(F32), XW, S.xgrad, XC)
        slot = S.xgrad.at[i, block(x, y)]
        st.xown_y[i] = go(remote(slot, slot, to_y))
        st.xown_p[i] = go(remote(slot, slot, to_xp))
        st.xown_m[i] = go(remote(slot, slot, to_xm))
        for s in (0, 1):
            st.yfd[i, 1, s].wait_recv()
            st.yc[i, s].wait_recv()
        total = (
            S.ysum[i, quarter(x), :] + S.yfd_r[i, 1].astype(F32) + S.yc_r[i].astype(F32)
        )
        activate(i, total, YW, S.ygrad, YC)
        slot = S.ygrad.at[i, block(x, y)]
        st.yown_p[i] = go(remote(slot, slot, to_xp))
        st.yown_m[i] = go(remote(slot, slot, to_xm))
        st.yown_y[i] = go(remote(slot, slot, to_y))

    def b2(i):
        st.xown_y[i].wait_recv()
        slot = S.xgrad.at[i, block(x, 1 - y)]
        st.xoth_p[i] = go(remote(slot, slot, to_xp))
        st.xoth_m[i] = go(remote(slot, slot, to_xm))
        left, right = pl.ds(0, YW), pl.ds(YW, YW)
        st.yown_p[i].wait_recv()
        part = S.ygrad.at[i, block(x_m, y), left]
        st.yfar_p[i] = go(remote(part, part, to_xp))
        slot = S.ygrad.at[i, block(x_m, y)]
        st.yy_m[i] = go(remote(slot, slot, to_y))
        st.yown_m[i].wait_recv()
        part = S.ygrad.at[i, block(x_p, y), right]
        st.yfar_m[i] = go(remote(part, part, to_xm))
        slot = S.ygrad.at[i, block(x_p, y)]
        st.yy_p[i] = go(remote(slot, slot, to_y))

    def b3(i):
        st.xown_p[i].wait_recv()
        slot = S.xgrad.at[i, block(x_m, y)]
        st.xfar_p[i] = go(remote(slot, slot, to_xp))
        st.xoth_m[i].wait_recv()
        slot = S.xgrad.at[i, block(x_p, 1 - y)]
        st.xfar_m[i] = go(remote(slot, slot, to_xm))
        st.yfar_p[i].wait_recv()
        st.yfar_m[i].wait_recv()
        slot = S.ygrad.at[i, block(x_f, y)]
        st.yy_f[i] = go(remote(slot, slot, to_y))

    def owner_core(i):
        return i % 2

    def owner_yh(i):
        return i // 2

    def b4(i):
        for copies in (st.xown_m, st.xoth_p, st.xfar_p, st.xfar_m):
            copies[i].wait_recv()
        v = dot_t(S.xgrad[i, :, 0:XW], S.gw[:, XC]) + dot_t(S.xgrad[i, :, XW:], S.uw[:, XC])
        S.acc[i] = v
        for copies in (st.yown_y, st.yy_m, st.yy_p, st.yy_f):
            copies[i].wait_recv()
        v = dot_t(S.ygrad[i, :, 0:YW], S.gw[:, YC]) + dot_t(S.ygrad[i, :, YW:], S.uw[:, YC])
        S.acc[i] += v
        st.core[i] = remote(S.acc.at[i], S.core_r.at[i], to_core)
        away = core != owner_core(i)

        @pl.when(away)
        def _():
            go(st.core[i], away)

    def z_rows(j):
        return pl.ds(pl.multiple_of(lax.rem(z + j, 8) * BLK, BLK), BLK)

    def c2(i):
        here = core == owner_core(i)
        for j in range(1, 8):
            dev = fsdp(lax.rem(f + 4 * j, 32))
            st.z[i, j] = remote(S.z_s.at[i, j], S.z_r.at[i, j], dev)

        @pl.when(here)
        def _():
            st.core[i].wait_recv()
            for j in (4, 3, 5, 2, 6, 1, 7):
                rows = z_rows(j)
                S.z_s[i, j] = (S.acc[i, rows, :] + S.core_r[i, rows, :]).astype(BF16)
                go(st.z[i, j], here)

    def c3(i):
        here = core == owner_core(i)
        away = jnp.logical_and(here, yh != owner_yh(i))
        st.yh[i] = remote(S.yh_s.at[i], S.yh_r.at[i], to_yh)

        @pl.when(here)
        def _():
            rows = z_rows(0)
            total = S.acc[i, rows, :] + S.core_r[i, rows, :]
            for j in (1, 7, 2, 6, 3, 5, 4):
                st.z[i, j].wait_recv()
                total = total + S.z_r[i, j].astype(F32)
            S.yh_s[i] = total

        @pl.when(away)
        def _():
            go(st.yh[i], away)

    def c4(i):
        @pl.when(jnp.logical_and(core == owner_core(i), yh == owner_yh(i)))
        def _():
            st.yh[i].wait_recv()
            gi_o[...] = (S.yh_s[i] + S.yh_r[i]).astype(BF16)

    def back_send():
        for b in range(8):
            rows = jnp.concatenate([S.back[i, b] for i in range(BATCHES)], axis=0)
            S.back_s[b] = pack(rows).astype(BF16)
        for j in range(1, 8):
            dst = lax.rem(p + j, 8)
            st.back[j] = go(remote(S.back_s.at[dst], S.back_r.at[j], pipe(dst)))

    def low_1():
        S.low_s[...] = pack(dot_t(S.hidden[...], S.down_a[...]))
        st.low_c[0] = go(remote(S.low_s, S.low_cr, to_core))
        total = S.back_s[p].astype(F32)
        for j in range(1, 8):
            st.back[j].wait_recv()
            total = total + S.back_r[j].astype(F32)
        back = (0.5 * unpack(total)).astype(BF16)
        S.la_s[...] = dot_lead(back, S.hidden[...])
        for j in range(1, 8):
            dst = lax.rem(p + j, 8)
            rows = S.la_s.at[pl.ds(pl.multiple_of(dst * 8, 8), 8)]
            st.la[j] = go(remote(rows, S.la_r.at[j], pipe(dst)))

    def low_2():
        st.low_c[0].wait_recv()
        rows = pl.ds(pl.multiple_of(core * 16, 16), 16)
        S.low_h[...] = S.low_s[rows, :] + S.low_cr[rows, :]
        for j in range(1, 16):
            dev = fsdp(lax.rem(chip + j, 16) * 2 + core)
            st.low_z[j] = go(remote(S.low_h, S.low_zr.at[j], dev))

    def la_2():
        mine = pl.ds(pl.multiple_of(p * 8, 8), 8)
        total = S.la_s[mine, :]
        for j in range(1, 8):
            st.la[j].wait_recv()
            total = total + S.la_r[j]
        S.la[mine, :] = total
        slot = S.la.at[mine]
        for j in range(1, 8):
            st.la_g[j] = go(remote(slot, slot, pipe(lax.rem(p + j, 8))))

    def low_3():
        total = S.low_h[...]
        for j in range(1, 16):
            st.low_z[j].wait_recv()
            total = total + S.low_zr[j]
        S.low_p[core, p] = total.astype(BF16)
        slot = S.low_p.at[core, p]
        for j in range(1, 8):
            st.low_p[j] = go(remote(slot, slot, pipe(lax.rem(p + j, 8))))

    def low_4():
        for j in range(1, 8):
            st.low_p[j].wait_recv()
        slot = S.low_p.at[core]
        st.low_g[0] = go(remote(slot, slot, to_core))

    def la_3():
        for j in range(1, 8):
            st.la_g[j].wait_recv()
        la_o[...] = S.la[...]

    def low_5():
        st.low_g[0].wait_recv()
        rows = []
        for b in range(8):
            v = jnp.concatenate([S.low_p[0, b], S.low_p[1, b]], axis=0).astype(F32)
            rows.append(unpack(v))
        total = None
        for i in range(BATCHES):
            low = jnp.concatenate([v[i * BLK : (i + 1) * BLK] for v in rows], axis=0)
            v = dot((0.5 * low).T.astype(BF16), whole(S.cot, i))
            total = v if total is None else total + v
        lb_o[...] = total

    a1(0)
    a1(1)
    a2(0)
    a1(2)
    a2(1)
    a3(0)
    a1(3)
    a2(2)
    a3(1)
    a4(0)
    back_send()
    a2(3)
    a3(2)
    a4(1)
    b2(0)
    a3(3)
    a4(2)
    b2(1)
    b3(0)
    a4(3)
    b2(2)
    b3(1)
    b4(0)
    b2(3)
    b3(2)
    low_1()
    b4(1)
    c2(0)
    b3(3)
    b4(2)
    low_2()
    c2(1)
    b4(3)
    c2(2)
    la_2()
    c3(0)
    low_3()
    c2(3)
    c3(1)
    la_3()
    low_4()
    c4(0)
    c3(2)
    c4(1)
    low_5()
    c3(3)
    c4(2)
    c4(3)
    for cp, cond in sent:
        if cond is None:
            cp.wait_send()
        else:
            pl.when(cond)(cp.wait_send)


def hand_over(*refs):
    for src, dst in zip(refs[:3], refs[3:]):
        dst[...] = src[...]


def shards(tok, cot, gate_w, up_w, down_w, down_a, down_b):
    any_ = pl.BlockSpec(memory_space=pl.ANY)
    vmem = pl.BlockSpec(memory_space=pltpu.VMEM)
    grad_in, grad_a, grad_b = pl.pallas_call(
        kernel,
        out_shape=(
            jax.ShapeDtypeStruct((16, FEAT), BF16),
            jax.ShapeDtypeStruct((RANK, HID), F32),
            jax.ShapeDtypeStruct((RANK, FEAT), F32),
        ),
        in_specs=[any_] * 7,
        out_specs=(vmem, vmem, vmem),
        scratch_shapes=scratch_spec()[0]
        + [
            pltpu.SemaphoreType.DMA((N_COPIES,)),
            pltpu.SemaphoreType.DMA((N_COPIES,)),
            pltpu.SemaphoreType.DMA((N_LOADS,)),
        ],
        compiler_params=pltpu.CompilerParams(
            collective_id=0, has_side_effects=True, vmem_limit_bytes=60 * 2**20
        ),
    )(tok.reshape(8, 4, BLK, FEAT), cot.reshape(8, 4, BLK, FEAT), gate_w, up_w, down_w, down_a.T, down_b)
    grad_in, grad_a, grad_b = pl.pallas_call(
        hand_over,
        out_shape=(
            jax.ShapeDtypeStruct((16, FEAT), BF16),
            jax.ShapeDtypeStruct((RANK, HID), F32),
            jax.ShapeDtypeStruct((RANK, FEAT), F32),
        ),
        in_specs=[vmem] * 3,
        out_specs=(vmem, vmem, vmem),
    )(grad_in, grad_a, grad_b)
    return grad_in, grad_a.T, grad_b


def solution(mesh):
    return jax.shard_map(
        shards,
        mesh=mesh,
        in_specs=(
            P(None, "pipe"),
            P(None, "pipe"),
            P("pipe", "fsdp"),
            P("pipe", "fsdp"),
            P("fsdp", "pipe"),
            P("fsdp", None),
            P(None, "pipe"),
        ),
        out_specs=(P("fsdp", "pipe"), P("fsdp", None), P(None, "pipe")),
        check_vma=False,
    )
```

time: 319 us -> 79.6 us (0.25); the launches traced: 314 us -> 79.5 us
  blocking collectives: 168 us -> 0 us
  waiting for transfers between devices: 99.3 us -> 0 us
  Pallas kernels: 0 us -> 78.8 us
  matrix products: 26.6 us -> 0 us
  between operations: 14.1 us -> 0.64 us
  other arithmetic: 4.09 us -> 0 us
    psum x2 -> x0, blocking collectives: 168 us -> none  [the longest x1 130 us: shards(): lowrank_product = lax.psum(lowrank_piece, 'fsdp').astype(jnp.bfloat16)]
    psum x1 -> x0, waiting for transfers between devices: 99.2 us -> none  [shards(): gate, up_values = lax.psum((gate_part, up_part), 'pipe')]
    pallas_call x0 -> x2, Pallas kernels: none -> 78.8 us  [the longest x1 76.8 us: shards(): pl.pallas_call(kernel, out_shape=(jax.ShapeDtypeStruct((16, FEAT), BF16),...]
    dot_general x10 -> x0, matrix products: 26.6 us -> none  [the longest x5 13 us: contract_trailing(): lax.dot_general(left, right, (((1,), (1,)), ((), ())), preferred_element_...]
    convert_element_type x2 -> x0, other arithmetic: 4.09 us -> none  [the longest x1 2.57 us: activate(): (silu_gate * up_values).astype(jnp.bfloat16)]
  transfers between devices with their start and end apart: 2 -> 0, of which waited for: 1 -> 0; matrix products, arithmetic and copies ran while one was open for 3% -> 0% of each run, Pallas kernels for 0% -> 0%
where the time goes in v1:
time: 79.6 us; the launch traced here: 79.5 us
  Pallas kernels  78.8 us (99%)
    pallas_call x1, Pallas kernels, shards(): pl.pallas_call(kernel, out_shape=(jax.ShapeDtypeStruct((16, FEAT), BF16),...  76.8 us
    pallas_call x1, Pallas kernels, shards(): pl.pallas_call(hand_over, out_shape=(jax.ShapeDtypeStruct((16, FEAT), BF1...  2 us

profile of v1, /device:TPU:24, one launch (start us, length us, event | category | flops | bytes accessed | tf_op | source)
XLA Modules:
  0.0 79.5 jit_solution(17668238758754243893)
XLA Ops:
  0.6 76.8 %shard_map.94 = (bf16[16,1536]{1,0:T(8,128)(2,1)}, f32[64,896]{1,0:T(8,128)}, f32[64,1536]{1,0:T(8,128)}) custom-call(bf16[8,4,16,1536]{3,2,1,0:T(8,128)(2,1)} %bitcast.4, bf16[8,4,16,1536]{3,2,1,0:T(8,128)(2,1)} %bitcast.5, bf16[1536,896]{1,0:T(8,128)(2,1)} %refs_2_.1, bf16[1536,896]{1,0:T(8,128)(2,1)} %refs_3_.1, bf16[896,1536]{1,0:T(8,128)(2,1)} %refs_4_.1, ...), custom_call_target="tpu_custom_call" | custom-call | tf_op jit(solution)/shard_map/pallas_call | solution.py:543
  77.5 2.0 %shard_map.95 = (bf16[16,1536]{1,0:T(8,128)(2,1)}, f32[64,896]{1,0:T(8,128)}, f32[64,1536]{1,0:T(8,128)}) custom-call(bf16[16,1536]{1,0:T(8,128)(2,1)} %get-tuple-element.9.refs_0_, f32[64,896]{1,0:T(8,128)} %get-tuple-element.10.refs_1_, f32[64,1536]{1,0:T(8,128)} %get-tuple-element.11.refs_2_), custom_call_target="tpu_custom_call" | custom-call | tf_op jit(solution)/shard_map/pallas_call | solution.py:562

commit v2 on v1

--- a/solution.py
+++ b/solution.py
@@ -19,7 +19,7 @@
 XW = 512
 YW = 384
 SPLIT = (0, 640, 1152)
-N_COPIES = 200
+N_COPIES = 240
 N_LOADS = 20
 
 
@@ -52,6 +52,10 @@
         made = {}
         setattr(self, name, made)
         return made
+
+
+def n_parts(i):
+    return 2 if i == BATCHES - 1 else 1
 
 
 def scratch_spec():
@@ -157,7 +161,12 @@
             device_id_type=MESH,
         )
 
+    entered = []
+
     def go(cp, cond=None):
+        if not entered:
+            pl.semaphore_wait(barrier, len(peers))
+            entered.append(True)
         cp.start()
         sent.append((cp, cond))
         return cp
@@ -220,35 +229,43 @@
         back = (0.5 * S.back[i].reshape(ROWS, RANK)).astype(BF16)
         part[i, :, 2 * w :] = dot_t(cot, S.dw[cols, :]) + dot(back, S.down_a[:, cols])
 
-    def a1(i):
-        if i == 0:
-            for key in ((TOKENS, 0), (COT, 0), DOWN_A, DOWN_B):
+    waited = set()
+
+    def need(*keys):
+        for key in keys:
+            if key not in waited:
+                waited.add(key)
                 loads[key].wait()
-            for kind in (GATE_W, UP_W, DOWN_W):
-                loads[kind, 0].wait()
-        else:
-            loads[TOKENS, i].wait()
-            loads[COT, i].wait()
-        S.back[i] = dot_t(whole(S.cot, i), S.down_b[...]).reshape(8, BLK, RANK)
+
+    def back_of(i):
+        need((COT, i), DOWN_B)
+        if (RANK, i) not in waited:
+            waited.add((RANK, i))
+            S.back[i] = dot_t(whole(S.cot, i), S.down_b[...]).reshape(8, BLK, RANK)
+
+    def a1x(i):
+        need((TOKENS, i), (GATE_W, 0), (UP_W, 0), (DOWN_W, 0), DOWN_A)
+        back_of(i)
         products(i, S.xpart, XC, XW)
-        if i == 0:
-            pl.semaphore_wait(barrier, len(peers))
         plan = ((x_f, 0, to_xp), (x_f, 1, to_xm), (x_p, 1, to_xp), (x_m, 0, to_xm))
         for k, (bx, by, dev) in enumerate(plan):
             S.xfd_s[i, k] = S.xpart[i, block(bx, by), :].astype(BF16)
             st.xfd[i, k] = go(remote(S.xfd_s.at[i, k], S.xfd_r.at[i, k], dev))
-        if i == 0:
-            for kind in (GATE_W, UP_W, DOWN_W):
-                loads[kind, 1].wait()
+
+    def a1y(i):
+        need((TOKENS, i), (GATE_W, 1), (UP_W, 1), (DOWN_W, 1), DOWN_A)
+        back_of(i)
         products(i, S.ypart, YC, YW)
         S.yy_s[i] = S.ypart[i, half(1 - y), :].astype(BF16)
         st.yy[i] = go(remote(S.yy_s.at[i], S.yy_r.at[i], to_y))
 
-    def a2(i):
+    def a2x(i):
         for k, rows, dev in ((0, block(x_p, 0), to_xp), (1, block(x_m, 1), to_xm)):
             st.xfd[i, k].wait_recv()
             S.xc_s[i, k] = (S.xpart[i, rows, :] + S.xfd_r[i, k].astype(F32)).astype(BF16)
             st.xc[i, k] = go(remote(S.xc_s.at[i, k], S.xc_r.at[i, k], dev))
+
+    def a2y(i):
         st.yy[i].wait_recv()
         S.ysum[i] = S.ypart[i, half(y), :] + S.yy_r[i].astype(F32)
         plan = ((0, 0, x_f, to_xp), (0, 1, x_f, to_xm), (1, 1, x_p, to_xp), (1, 0, x_m, to_xm))
@@ -260,7 +277,7 @@
                 )
             )
 
-    def a3(i):
+    def a3x(i):
         for k in (2, 3):
             st.xfd[i, k].wait_recv()
         for k in (0, 1):
@@ -273,6 +290,8 @@
             )
         S.xy_s[i] = S.xsum[i, 1 - y].astype(BF16)
         st.xy[i] = go(remote(S.xy_s.at[i], S.xy_r.at[i], to_y))
+
+    def a3y(i):
         for s, bx, dev in ((0, x_p, to_xp), (1, x_m, to_xm)):
             st.yfd[i, 0, s].wait_recv()
             S.yc_s[i, :, side(s)] = (
@@ -291,13 +310,15 @@
         grad[i, mine, w : 2 * w] = (hg * silu).astype(BF16)
         S.hidden[i * BLK : (i + 1) * BLK, cols] = (silu * up).astype(BF16)
 
-    def a4(i):
+    def a4x(i):
         st.xy[i].wait_recv()
         activate(i, S.xsum[i, y] + S.xy_r[i].astype(F32), XW, S.xgrad, XC)
         slot = S.xgrad.at[i, block(x, y)]
         st.xown_y[i] = go(remote(slot, slot, to_y))
         st.xown_p[i] = go(remote(slot, slot, to_xp))
         st.xown_m[i] = go(remote(slot, slot, to_xm))
+
+    def a4y(i):
         for s in (0, 1):
             st.yfd[i, 1, s].wait_recv()
             st.yc[i, s].wait_recv()
@@ -310,11 +331,13 @@
         st.yown_m[i] = go(remote(slot, slot, to_xm))
         st.yown_y[i] = go(remote(slot, slot, to_y))
 
-    def b2(i):
+    def b2x(i):
         st.xown_y[i].wait_recv()
         slot = S.xgrad.at[i, block(x, 1 - y)]
         st.xoth_p[i] = go(remote(slot, slot, to_xp))
         st.xoth_m[i] = go(remote(slot, slot, to_xm))
+
+    def b2y(i):
         left, right = pl.ds(0, YW), pl.ds(YW, YW)
         st.yown_p[i].wait_recv()
         part = S.ygrad.at[i, block(x_m, y), left]
@@ -327,13 +350,15 @@
         slot = S.ygrad.at[i, block(x_p, y)]
         st.yy_p[i] = go(remote(slot, slot, to_y))
 
-    def b3(i):
+    def b3x(i):
         st.xown_p[i].wait_recv()
         slot = S.xgrad.at[i, block(x_m, y)]
         st.xfar_p[i] = go(remote(slot, slot, to_xp))
         st.xoth_m[i].wait_recv()
         slot = S.xgrad.at[i, block(x_p, 1 - y)]
         st.xfar_m[i] = go(remote(slot, slot, to_xm))
+
+    def b3y(i):
         st.yfar_p[i].wait_recv()
         st.yfar_m[i].wait_recv()
         slot = S.ygrad.at[i, block(x_f, y)]
@@ -345,62 +370,74 @@
     def owner_yh(i):
         return i // 2
 
-    def b4(i):
+    def part_cols(i, q):
+        w = FEAT // n_parts(i)
+        return slice(q * w, (q + 1) * w), pl.ds(q * w, w)
+
+    def b4x(i):
         for copies in (st.xown_m, st.xoth_p, st.xfar_p, st.xfar_m):
             copies[i].wait_recv()
         v = dot_t(S.xgrad[i, :, 0:XW], S.gw[:, XC]) + dot_t(S.xgrad[i, :, XW:], S.uw[:, XC])
         S.acc[i] = v
+
+    def b4y(i):
         for copies in (st.yown_y, st.yy_m, st.yy_p, st.yy_f):
             copies[i].wait_recv()
-        v = dot_t(S.ygrad[i, :, 0:YW], S.gw[:, YC]) + dot_t(S.ygrad[i, :, YW:], S.uw[:, YC])
-        S.acc[i] += v
-        st.core[i] = remote(S.acc.at[i], S.core_r.at[i], to_core)
         away = core != owner_core(i)
-
-        @pl.when(away)
-        def _():
-            go(st.core[i], away)
+        for q in range(n_parts(i)):
+            cols, cols_d = part_cols(i, q)
+            S.acc[i, :, cols] += dot_t(S.ygrad[i, :, 0:YW], S.gw[cols, YC]) + dot_t(
+                S.ygrad[i, :, YW:], S.uw[cols, YC]
+            )
+            st.core[i, q] = remote(S.acc.at[i, :, cols_d], S.core_r.at[i, :, cols_d], to_core)
+            pl.when(away)(lambda q=q: go(st.core[i, q], away) and None)
 
     def z_rows(j):
         return pl.ds(pl.multiple_of(lax.rem(z + j, 8) * BLK, BLK), BLK)
 
-    def c2(i):
+    def c2(i, q=0):
         here = core == owner_core(i)
+        cols, cols_d = part_cols(i, q)
         for j in range(1, 8):
             dev = fsdp(lax.rem(f + 4 * j, 32))
-            st.z[i, j] = remote(S.z_s.at[i, j], S.z_r.at[i, j], dev)
+            st.z[i, q, j] = remote(S.z_s.at[i, j, :, cols_d], S.z_r.at[i, j, :, cols_d], dev)
 
         @pl.when(here)
         def _():
-            st.core[i].wait_recv()
+            st.core[i, q].wait_recv()
             for j in (4, 3, 5, 2, 6, 1, 7):
                 rows = z_rows(j)
-                S.z_s[i, j] = (S.acc[i, rows, :] + S.core_r[i, rows, :]).astype(BF16)
-                go(st.z[i, j], here)
-
-    def c3(i):
+                S.z_s[i, j, :, cols] = (
+                    S.acc[i, rows, cols] + S.core_r[i, rows, cols]
+                ).astype(BF16)
+                go(st.z[i, q, j], here)
+
+    def c3(i, q=0):
         here = core == owner_core(i)
         away = jnp.logical_and(here, yh != owner_yh(i))
-        st.yh[i] = remote(S.yh_s.at[i], S.yh_r.at[i], to_yh)
+        cols, cols_d = part_cols(i, q)
+        st.yh[i, q] = remote(S.yh_s.at[i, :, cols_d], S.yh_r.at[i, :, cols_d], to_yh)
 
         @pl.when(here)
         def _():
             rows = z_rows(0)
-            total = S.acc[i, rows, :] + S.core_r[i, rows, :]
+            total = S.acc[i, rows, cols] + S.core_r[i, rows, cols]
             for j in (1, 7, 2, 6, 3, 5, 4):
-                st.z[i, j].wait_recv()
-                total = total + S.z_r[i, j].astype(F32)
-            S.yh_s[i] = total
+                st.z[i, q, j].wait_recv()
+                total = total + S.z_r[i, j, :, cols].astype(F32)
+            S.yh_s[i, :, cols] = total
 
         @pl.when(away)
         def _():
-            go(st.yh[i], away)
-
-    def c4(i):
+            go(st.yh[i, q], away)
+
+    def c4(i, q=0):
+        cols, _ = part_cols(i, q)
+
         @pl.when(jnp.logical_and(core == owner_core(i), yh == owner_yh(i)))
         def _():
-            st.yh[i].wait_recv()
-            gi_o[...] = (S.yh_s[i] + S.yh_r[i]).astype(BF16)
+            st.yh[i, q].wait_recv()
+            gi_o[:, cols] = (S.yh_s[i, :, cols] + S.yh_r[i, :, cols]).astype(BF16)
 
     def back_send():
         for b in range(8):
@@ -411,8 +448,10 @@
             st.back[j] = go(remote(S.back_s.at[dst], S.back_r.at[j], pipe(dst)))
 
     def low_1():
-        S.low_s[...] = pack(dot_t(S.hidden[...], S.down_a[...]))
+        S.low_s[...] = pack(dot_t(S.down_a[...], S.hidden[...]))
         st.low_c[0] = go(remote(S.low_s, S.low_cr, to_core))
+
+    def la_1():
         total = S.back_s[p].astype(F32)
         for j in range(1, 8):
             st.back[j].wait_recv()
@@ -466,65 +505,94 @@
 
     def low_5():
         st.low_g[0].wait_recv()
-        rows = []
+        total = None
         for b in range(8):
             v = jnp.concatenate([S.low_p[0, b], S.low_p[1, b]], axis=0).astype(F32)
-            rows.append(unpack(v))
-        total = None
-        for i in range(BATCHES):
-            low = jnp.concatenate([v[i * BLK : (i + 1) * BLK] for v in rows], axis=0)
-            v = dot((0.5 * low).T.astype(BF16), whole(S.cot, i))
+            low = (0.5 * unpack(v)).astype(BF16)
+            v = dot(low, S.cot[:, b].reshape(64, FEAT))
             total = v if total is None else total + v
         lb_o[...] = total
 
-    a1(0)
-    a1(1)
-    a2(0)
-    a1(2)
-    a2(1)
-    a3(0)
-    a1(3)
-    a2(2)
-    a3(1)
-    a4(0)
+    a1x(0)
+    a1y(1)
+    a1x(2)
+    a1y(0)
+    a2x(0)
+    a1x(1)
+    a1y(2)
+    a2x(2)
+    a1x(3)
+    a2y(0)
+    a3x(0)
+    a1y(3)
+    a2x(1)
+    a2y(1)
+    a3y(0)
+    a2x(3)
+    a4x(0)
+    a2y(2)
+    a3x(1)
+    a4y(0)
+    a3x(2)
+    a2y(3)
+    a3y(1)
+    b2x(0)
+    a3x(3)
+    a4x(1)
+    b2y(0)
+    a3y(3)
+    a3y(2)
+    a4y(1)
+    b3x(0)
+    a4x(2)
+    b2x(1)
+    b3y(0)
+    a4x(3)
+    a4y(3)
+    a4y(2)
+    low_1()
+    b2y(1)
+    b4x(0)
+    b2x(2)
+    b4y(0)
+    b3x(1)
+    low_2()
+    b2x(3)
+    b3y(1)
+    b2y(2)
+    b2y(3)
+    c2(0)
+    b3x(2)
+    b4x(1)
+    b4y(1)
+    b3x(3)
+    b3y(2)
     back_send()
-    a2(3)
-    a3(2)
-    a4(1)
-    b2(0)
-    a3(3)
-    a4(2)
-    b2(1)
-    b3(0)
-    a4(3)
-    b2(2)
-    b3(1)
-    b4(0)
-    b2(3)
-    b3(2)
-    low_1()
-    b4(1)
-    c2(0)
-    b3(3)
-    b4(2)
-    low_2()
+    b3y(3)
+    b4x(2)
     c2(1)
-    b4(3)
+    b4y(2)
+    b4x(3)
+    low_3()
     c2(2)
+    c3(0)
+    la_1()
+    b4y(3)
+    c2(3, 0)
+    c4(0)
+    c3(1)
     la_2()
-    c3(0)
-    low_3()
-    c2(3)
-    c3(1)
+    c2(3, 1)
+    low_4()
+    c4(1)
+    c3(2)
+    c3(3, 0)
+    c3(3, 1)
+    c4(2)
     la_3()
-    low_4()
-    c4(0)
-    c3(2)
-    c4(1)
     low_5()
-    c3(3)
-    c4(2)
-    c4(3)
+    c4(3, 0)
+    c4(3, 1)
     for cp, cond in sent:
         if cond is None:
             cp.wait_send()

time: 79.6 us -> 73.1 us (0.918)
  Pallas kernels: 78.8 us -> 72.3 us
    pallas_call x1, Pallas kernels: 76.8 us -> 70.3 us  [shards(): pl.pallas_call(kernel, out_shape=(jax.ShapeDtypeStruct((16, FEAT), BF16),...]
where the time goes in v2:
time: 73.1 us; the launch traced here: 73 us
  Pallas kernels  72.3 us (99%)
    pallas_call x1, Pallas kernels, shards(): pl.pallas_call(kernel, out_shape=(jax.ShapeDtypeStruct((16, FEAT), BF16),...  70.3 us
    pallas_call x1, Pallas kernels, shards(): pl.pallas_call(hand_over, out_shape=(jax.ShapeDtypeStruct((16, FEAT), BF1...  2 us

profile of v2, /device:TPU:24, one launch (start us, length us, event | category | flops | bytes accessed | tf_op | source)
XLA Modules:
  0.0 73.0 jit_solution(18274614282776996834)
XLA Ops:
  0.6 70.3 %shard_map.94 = (bf16[16,1536]{1,0:T(8,128)(2,1)}, f32[64,896]{1,0:T(8,128)}, f32[64,1536]{1,0:T(8,128)}) custom-call(bf16[8,4,16,1536]{3,2,1,0:T(8,128)(2,1)} %bitcast.4, bf16[8,4,16,1536]{3,2,1,0:T(8,128)(2,1)} %bitcast.5, bf16[1536,896]{1,0:T(8,128)(2,1)} %refs_2_.1, bf16[1536,896]{1,0:T(8,128)(2,1)} %refs_3_.1, bf16[896,1536]{1,0:T(8,128)(2,1)} %refs_4_.1, ...), custom_call_target="tpu_custom_call" | custom-call | tf_op jit(solution)/shard_map/pallas_call | solution.py:611
  71.0 2.0 %shard_map.95 = (bf16[16,1536]{1,0:T(8,128)(2,1)}, f32[64,896]{1,0:T(8,128)}, f32[64,1536]{1,0:T(8,128)}) custom-call(bf16[16,1536]{1,0:T(8,128)(2,1)} %get-tuple-element.9.refs_0_, f32[64,896]{1,0:T(8,128)} %get-tuple-element.10.refs_1_, f32[64,1536]{1,0:T(8,128)} %get-tuple-element.11.refs_2_), custom_call_target="tpu_custom_call" | custom-call | tf_op jit(solution)/shard_map/pallas_call | solution.py:630

commit v3 on v2

--- a/solution.py
+++ b/solution.py
@@ -19,7 +19,7 @@
 XW = 512
 YW = 384
 SPLIT = (0, 640, 1152)
-N_COPIES = 240
+N_COPIES = 260
 N_LOADS = 20
 
 
@@ -69,8 +69,8 @@
     n = BATCHES
     v.tok = new((n, 8, BLK, FEAT), BF16)
     v.cot = new((n, 8, BLK, FEAT), BF16)
-    v.gw = new((FEAT, HID), BF16)
-    v.uw = new((FEAT, HID), BF16)
+    v.wx = new((FEAT, 2 * XW), BF16)
+    v.wy = new((FEAT, 2 * YW), BF16)
     v.dw = new((HID, FEAT), BF16)
     v.down_a = new((RANK, HID), BF16)
     v.down_b = new((RANK, FEAT), BF16)
@@ -110,6 +110,7 @@
     v.core_r = new((n, ROWS, FEAT), F32)
     v.z_s = new((n, 8, BLK, FEAT), BF16)
     v.z_r = new((n, 8, BLK, FEAT), BF16)
+    v.other_r = new((n, 8, BLK, FEAT), BF16)
     v.yh_s = new((n, BLK, FEAT), F32)
     v.yh_r = new((n, BLK, FEAT), F32)
     return specs, v
@@ -182,14 +183,14 @@
     xcols, ycols = pl.ds(0, XW), pl.ds(XW, YW)
     TOKENS, COT, GATE_W, UP_W, DOWN_W, DOWN_A, DOWN_B = range(7)
     load((TOKENS, 0), S.tok.at[0], tok_h.at[:, 0])
-    load((GATE_W, 0), S.gw.at[:, xcols], gw_h.at[:, xcols])
-    load((UP_W, 0), S.uw.at[:, xcols], uw_h.at[:, xcols])
+    load((GATE_W, 0), S.wx.at[:, pl.ds(0, XW)], gw_h.at[:, xcols])
+    load((UP_W, 0), S.wx.at[:, pl.ds(XW, XW)], uw_h.at[:, xcols])
     load((COT, 0), S.cot.at[0], cot_h.at[:, 0])
     load(DOWN_B, S.down_b, b_h)
     load(DOWN_A, S.down_a, a_h)
     load((DOWN_W, 0), S.dw.at[xcols], dw_h.at[xcols])
-    load((GATE_W, 1), S.gw.at[:, ycols], gw_h.at[:, ycols])
-    load((UP_W, 1), S.uw.at[:, ycols], uw_h.at[:, ycols])
+    load((GATE_W, 1), S.wy.at[:, pl.ds(0, YW)], gw_h.at[:, ycols])
+    load((UP_W, 1), S.wy.at[:, pl.ds(YW, YW)], uw_h.at[:, ycols])
     load((DOWN_W, 1), S.dw.at[ycols], dw_h.at[ycols])
     for i in range(1, BATCHES):
         load((TOKENS, i), S.tok.at[i], tok_h.at[:, i])
@@ -222,10 +223,9 @@
     def whole(ref, i):
         return ref[i].reshape(ROWS, FEAT)
 
-    def products(i, part, cols, w):
+    def products(i, part, weights, cols, w):
         tok, cot = whole(S.tok, i), whole(S.cot, i)
-        part[i, :, 0:w] = dot(tok, S.gw[:, cols])
-        part[i, :, w : 2 * w] = dot(tok, S.uw[:, cols])
+        part[i, :, 0 : 2 * w] = dot(tok, weights[...])
         back = (0.5 * S.back[i].reshape(ROWS, RANK)).astype(BF16)
         part[i, :, 2 * w :] = dot_t(cot, S.dw[cols, :]) + dot(back, S.down_a[:, cols])
 
@@ -246,7 +246,7 @@
     def a1x(i):
         need((TOKENS, i), (GATE_W, 0), (UP_W, 0), (DOWN_W, 0), DOWN_A)
         back_of(i)
-        products(i, S.xpart, XC, XW)
+        products(i, S.xpart, S.wx, XC, XW)
         plan = ((x_f, 0, to_xp), (x_f, 1, to_xm), (x_p, 1, to_xp), (x_m, 0, to_xm))
         for k, (bx, by, dev) in enumerate(plan):
             S.xfd_s[i, k] = S.xpart[i, block(bx, by), :].astype(BF16)
@@ -255,7 +255,7 @@
     def a1y(i):
         need((TOKENS, i), (GATE_W, 1), (UP_W, 1), (DOWN_W, 1), DOWN_A)
         back_of(i)
-        products(i, S.ypart, YC, YW)
+        products(i, S.ypart, S.wy, YC, YW)
         S.yy_s[i] = S.ypart[i, half(1 - y), :].astype(BF16)
         st.yy[i] = go(remote(S.yy_s.at[i], S.yy_r.at[i], to_y))
 
@@ -377,8 +377,7 @@
     def b4x(i):
         for copies in (st.xown_m, st.xoth_p, st.xfar_p, st.xfar_m):
             copies[i].wait_recv()
-        v = dot_t(S.xgrad[i, :, 0:XW], S.gw[:, XC]) + dot_t(S.xgrad[i, :, XW:], S.uw[:, XC])
-        S.acc[i] = v
+        S.acc[i] = dot_t(S.xgrad[i], S.wx[...])
 
     def b4y(i):
         for copies in (st.yown_y, st.yy_m, st.yy_p, st.yy_f):
@@ -386,9 +385,7 @@
         away = core != owner_core(i)
         for q in range(n_parts(i)):
             cols, cols_d = part_cols(i, q)
-            S.acc[i, :, cols] += dot_t(S.ygrad[i, :, 0:YW], S.gw[cols, YC]) + dot_t(
-                S.ygrad[i, :, YW:], S.uw[cols, YC]
-            )
+            S.acc[i, :, cols] += dot_t(S.ygrad[i], S.wy[cols, :])
             st.core[i, q] = remote(S.acc.at[i, :, cols_d], S.core_r.at[i, :, cols_d], to_core)
             pl.when(away)(lambda q=q: go(st.core[i, q], away) and None)
 
@@ -439,6 +436,54 @@
             st.yh[i, q].wait_recv()
             gi_o[:, cols] = (S.yh_s[i, :, cols] + S.yh_r[i, :, cols]).astype(BF16)
 
+    def c2_direct(i, q):
+        here = core == owner_core(i)
+        same = jnp.logical_and(here, yh == owner_yh(i))
+        other = jnp.logical_and(here, yh != owner_yh(i))
+        cols, cols_d = part_cols(i, q)
+        for j in range(8):
+            src = S.z_s.at[i, j, :, cols_d]
+            dev = lax.rem(f + 4 * j, 32)
+            if j:
+                st.z[i, q, 0, j] = remote(src, S.z_r.at[i, j, :, cols_d], fsdp(dev))
+            dev = fsdp(dev + 2 - 4 * yh)
+            st.z[i, q, 1, j] = remote(src, S.other_r.at[i, j, :, cols_d], dev)
+
+        @pl.when(here)
+        def _():
+            st.core[i, q].wait_recv()
+
+        def send(ring, j, cond):
+            rows = z_rows(j)
+            S.z_s[i, j, :, cols] = (
+                S.acc[i, rows, cols] + S.core_r[i, rows, cols]
+            ).astype(BF16)
+            go(st.z[i, q, ring, j], cond)
+
+        @pl.when(same)
+        def _():
+            for j in (4, 3, 5, 2, 6, 1, 7):
+                send(0, j, same)
+
+        @pl.when(other)
+        def _():
+            for j in (4, 3, 5, 2, 6, 1, 7, 0):
+                send(1, j, other)
+
+    def c3_direct(i, q):
+        cols, _ = part_cols(i, q)
+
+        @pl.when(jnp.logical_and(core == owner_core(i), yh == owner_yh(i)))
+        def _():
+            rows = z_rows(0)
+            total = S.acc[i, rows, cols] + S.core_r[i, rows, cols]
+            for j in (1, 7, 0, 2, 6, 3, 5, 4):
+                for ring in (0, 1) if j else (1,):
+                    st.z[i, q, ring, j].wait_recv()
+                    got = S.other_r[i, j, :, cols] if ring else S.z_r[i, j, :, cols]
+                    total = total + got.astype(F32)
+            gi_o[:, cols] = total.astype(BF16)
+
     def back_send():
         for b in range(8):
             rows = jnp.concatenate([S.back[i, b] for i in range(BATCHES)], axis=0)
@@ -522,20 +567,20 @@
     a1y(2)
     a2x(2)
     a1x(3)
+    a3x(0)
     a2y(0)
-    a3x(0)
     a1y(3)
     a2x(1)
     a2y(1)
     a3y(0)
+    a4x(0)
     a2x(3)
-    a4x(0)
+    a3x(1)
+    a3y(1)
     a2y(2)
-    a3x(1)
+    a3x(2)
     a4y(0)
-    a3x(2)
     a2y(3)
-    a3y(1)
     b2x(0)
     a3x(3)
     a4x(1)
@@ -559,6 +604,7 @@
     low_2()
     b2x(3)
     b3y(1)
+    back_send()
     b2y(2)
     b2y(3)
     c2(0)
@@ -567,32 +613,28 @@
     b4y(1)
     b3x(3)
     b3y(2)
-    back_send()
+    la_1()
+    b4x(2)
     b3y(3)
-    b4x(2)
     c2(1)
     b4y(2)
+    low_3()
     b4x(3)
-    low_3()
-    c2(2)
+    la_2()
+    c2_direct(2, 0)
+    b4y(3)
     c3(0)
-    la_1()
-    b4y(3)
-    c2(3, 0)
+    low_4()
+    c2_direct(3, 0)
+    c2_direct(3, 1)
+    low_5()
+    la_3()
+    c3(1)
     c4(0)
-    c3(1)
-    la_2()
-    c2(3, 1)
-    low_4()
+    c3_direct(2, 0)
+    c3_direct(3, 0)
     c4(1)
-    c3(2)
-    c3(3, 0)
-    c3(3, 1)
-    c4(2)
-    la_3()
-    low_5()
-    c4(3, 0)
-    c4(3, 1)
+    c3_direct(3, 1)
     for cp, cond in sent:
         if cond is None:
             cp.wait_send()

time: 73.1 us -> 71.5 us (0.978); the launches traced: 73 us -> 70.2 us
  Pallas kernels: 72.3 us -> 69.6 us
    pallas_call x1, Pallas kernels: 70.3 us -> 67.6 us  [shards(): pl.pallas_call(kernel, out_shape=(jax.ShapeDtypeStruct((16, FEAT), BF16),...]
where the time goes in v3:
time: 71.5 us; the launch traced here: 70.2 us
  Pallas kernels  69.6 us (97%)
    pallas_call x1, Pallas kernels, shards(): pl.pallas_call(kernel, out_shape=(jax.ShapeDtypeStruct((16, FEAT), BF16),...  67.6 us
    pallas_call x1, Pallas kernels, shards(): pl.pallas_call(hand_over, out_shape=(jax.ShapeDtypeStruct((16, FEAT), BF1...  2 us

profile of v3, /device:TPU:24, one launch (start us, length us, event | category | flops | bytes accessed | tf_op | source)
XLA Modules:
  0.0 70.2 jit_solution(13107285441570449965)
XLA Ops:
  0.6 67.6 %shard_map.94 = (bf16[16,1536]{1,0:T(8,128)(2,1)}, f32[64,896]{1,0:T(8,128)}, f32[64,1536]{1,0:T(8,128)}) custom-call(bf16[8,4,16,1536]{3,2,1,0:T(8,128)(2,1)} %bitcast.4, bf16[8,4,16,1536]{3,2,1,0:T(8,128)(2,1)} %bitcast.5, bf16[1536,896]{1,0:T(8,128)(2,1)} %refs_2_.1, bf16[1536,896]{1,0:T(8,128)(2,1)} %refs_3_.1, bf16[896,1536]{1,0:T(8,128)(2,1)} %refs_4_.1, ...), custom_call_target="tpu_custom_call" | custom-call | tf_op jit(solution)/shard_map/pallas_call | solution.py:653
  68.2 2.0 %shard_map.95 = (bf16[16,1536]{1,0:T(8,128)(2,1)}, f32[64,896]{1,0:T(8,128)}, f32[64,1536]{1,0:T(8,128)}) custom-call(bf16[16,1536]{1,0:T(8,128)(2,1)} %get-tuple-element.9.refs_0_, f32[64,896]{1,0:T(8,128)} %get-tuple-element.10.refs_1_, f32[64,1536]{1,0:T(8,128)} %get-tuple-element.11.refs_2_), custom_call_target="tpu_custom_call" | custom-call | tf_op jit(solution)/shard_map/pallas_call | solution.py:672
